TPU v7x, 512 devices: a whole 4x4x16 slice. The times are simulated.
512 devices in a mesh: rep: 16 (over y, x), dom: 32 (over z, core).
Axes of the slice: x: 4, y: 4, z: 16, core: 2. Of those that a mesh axis runs over, the one named last changes fastest.
Arguments:
- positions: float32 [16, 3, 32768], P('rep', None, 'dom'), may hold values from -6 to 6
- velocities: float32 [16, 3, 32768], P('rep', None, 'dom'), may hold values from -6 to 6
- charge: float32 [32768], P('dom'), may hold values from 0.5 to 2
- inverse_mass: float32 [32768], P('dom'), may hold values from 0.5 to 2
- pair_tiles: int32 [256, 6], P('dom'), may hold values from -1 to 11, as said below
- halo_tiles: int32 [32, 2, 2], P('dom'), may hold values from 0 to 7, as said below
- owners: int32 [256, 4], P('dom'), may hold values from 0 to 31, all different within a row; in each aligned block of 8 rows (0 to 7, 8 to 15, ...) at most 2 rows name the same one
- centres: float32 [3, 32768], P(None, 'dom'), may hold values from -6 to 6
- widths: float32 [32768], P('dom'), may hold values from 1 to 4
- map_density: float32 [32768], P('dom'), may hold values from 0.1 to 0.6
- map_error: float32 [32768], P('dom'), may hold values from 0.1 to 0.3
- partner: int32 [16], replicated, may hold values from 0 to 15, as said below
- decision: int32 [16], replicated, may hold values from 0 to 1, as said below
Outputs:
- new_positions: float32 [16, 3, 32768], P('rep', None, 'dom')
- new_velocities: float32 [16, 3, 32768], P('rep', None, 'dom')
- model_map: float32 [32768], P('dom')
Inputs may be any that keep to these rules, and one draw needn't show every extreme that they name: `pair_tiles`: entry j of a tile's row names tile j of the same domain if j < 8; tile j - 8 of the upper list (row [d - 1, 1]) of the domain below if j < 10; else tile j - 10 of the lower list (row [d + 1, 0]) of the domain above; domains wrap around. -1 marks an empty entry; live entries of a row are distinct and come first. `halo_tiles`: row [d, 0] lists distinct tiles of domain d for domain d - 1, row [d, 1] distinct tiles for domain d + 1. `owners`: each row names 4 distinct domains; within the 8 rows of one domain no domain is named more than 2 times, a bound that some block reaches. `partner`: a permutation of the replicas; some replica r has partner r + 16 / 2 (counted round) and decision 1. `decision`: the same on all replicas of one cycle of partner; at least one replica is accepted and one is not.
All inputs are finite; a program needn't handle non-finite values.
Results may differ from a plain program's by a relative error of at most 0.0001.
Values sent between devices are 32-bit elements; how exact they have to be, the bound alone decides.
A program may use at most 64 MiB of HBM per device.

v0:
```python
import jax
import jax.numpy as jnp
from jax import lax
from jax.sharding import PartitionSpec as P

STEPS = 2


highest = lax.Precision.HIGHEST
time_step = 0.5
pair_width = 1.0
map_scale = 2.0


def with_halo(block, sides, width):
    for axis, dim in sides:
        count = lax.axis_size(axis)
        forward = [(i, i + 1) for i in range(count - 1)]
        forward.append((count - 1, 0))
        backward = [(target, source) for source, target in forward]
        low = lax.ppermute(
            lax.slice_in_dim(block, block.shape[dim] - width, None, axis=dim), axis, forward
        )
        high = lax.ppermute(lax.slice_in_dim(block, 0, width, axis=dim), axis, backward)
        block = jnp.concatenate([low, block, high], axis=dim)
    return block


def block_size(count, wanted):
    size = max(1, min(count, wanted))
    while count % size:
        size = size - 1
    return size


def pair_force(own_tiles, neighbours, pair_gain):
    squared = jnp.zeros(
        neighbours.shape[:2] + (own_tiles.shape[2], neighbours.shape[3]), jnp.float32
    )
    for dim_index in range(3):
        apart = own_tiles[:, None, dim_index, :, None] - neighbours[:, :, dim_index, None, :]
        squared = squared + apart * apart
    weights = jnp.exp(-squared / (2.0 * pair_width)) * neighbours[:, :, 3, None, :]
    weight_sum = jnp.sum(weights, (1, 3))
    pulled = jnp.einsum("bjat,bjct->bca", weights, neighbours[:, :, :3, :], precision=highest)
    return (
        pair_gain
        / pair_width
        * own_tiles[:, 3, None, :]
        * (own_tiles[:, :3, :] * weight_sum[:, None, :] - pulled)
    )


def slot_gaussians(coords, centre, extent):
    squared = jnp.zeros((coords.shape[0], coords.shape[2], centre.shape[1]), jnp.float32)
    for dim_index in range(3):
        apart = coords[:, dim_index, :, None] - centre[dim_index][None, None, :]
        squared = squared + apart * apart
    return jnp.exp(-squared / (2.0 * extent[None, None, :]))


def owner_matrix(owners, domains, capacity):
    tile_count, owned = owners.shape
    flat_owners = owners.reshape(-1)
    matches = (flat_owners[:, None] == jnp.arange(domains, dtype=jnp.int32)[None, :]).astype(
        jnp.int32
    )
    earlier = jnp.cumsum(matches, 0) - matches
    slot_ids = jnp.sum(earlier * matches, 1)
    targets = (flat_owners * capacity + slot_ids).reshape(tile_count, owned)
    row_ids = jnp.arange(domains * capacity, dtype=jnp.int32)
    return jnp.sum((row_ids[:, None, None] == targets[None, :, :]).astype(jnp.float32), 2)


def nonbonded(position, charges, halo_tiles, pair_tiles):
    tile_count = position.shape[0]
    tile_len = position.shape[2]
    stacked = jnp.concatenate([position, charges[:, None, :]], 1)
    halo_sides = halo_tiles[0]
    side_select = (
        halo_sides[:, :, None] == jnp.arange(tile_count, dtype=jnp.int32)[None, None, :]
    ).astype(jnp.float32)
    rim_out = jnp.einsum("shn,nck->shck", side_select, stacked, precision=highest)
    padded = with_halo(rim_out, (("dom", 0),), 1)
    tile_table = jnp.concatenate([stacked, padded[0], padded[3]], 0)
    extent = tile_table.shape[0]
    selection = (
        pair_tiles[:, :, None] == jnp.arange(extent, dtype=jnp.int32)[None, None, :]
    ).astype(jnp.float32)
    near_tiles = jnp.einsum("njw,wck->njck", selection, tile_table, precision=highest)
    group_size = block_size(tile_count, max(1, 512 // tile_len))
    pair_gain = (pair_tiles.shape[1] * tile_len) ** (-0.5)

    def one_block(pieces):
        return pair_force(pieces[0], pieces[1], pair_gain)

    shaped = (
        stacked.reshape((-1, group_size) + stacked.shape[1:]),
        near_tiles.reshape((-1, group_size) + near_tiles.shape[1:]),
    )
    return lax.map(one_block, shaped).reshape(tile_count, 3, tile_len)


def map_send(position, owners, centre, extent, density, error, intersection_scale):
    domains = lax.axis_size("dom")
    tile_count, owned = owners.shape
    tile_len = position.shape[2]
    map_gain = map_scale / (owned * centre.shape[1])
    capacity = max(2, tile_count * owned // domains + 1)
    matrix = owner_matrix(owners, domains, capacity)
    outgoing = jnp.einsum("sn,nck->sck", matrix, position, precision=highest).reshape(
        domains, capacity, 3, tile_len
    )
    live_slots = jnp.sum(matrix, 1).reshape(domains, capacity)
    arrived, alive_flags = (
        lax.all_to_all(outgoing, "dom", split_axis=0, concat_axis=0, tiled=True),
        lax.all_to_all(live_slots, "dom", split_axis=0, concat_axis=0, tiled=True),
    )
    slot_total = domains * capacity
    group_size = block_size(slot_total, max(1, 512 // tile_len))
    coords_block = arrived.reshape(-1, group_size, 3, tile_len)
    alive_blocks = alive_flags.reshape(-1, group_size)

    def intersection_pass(pieces):
        return jnp.sum(slot_gaussians(pieces[0], centre, extent) * pieces[1][:, None, None], (0, 1))

    partial_value = (
        jnp.sum(lax.map(intersection_pass, (coords_block, alive_blocks)), 0) * intersection_scale
    )
    totals = lax.psum(partial_value, "rep")
    model_map = totals / lax.axis_size("rep")
    coefficient = map_gain * (model_map - density) / (error * error) / extent

    def force_pass(pieces):
        weighted = (
            slot_gaussians(pieces[0], centre, extent)
            * coefficient[None, None, :]
            * pieces[1][:, None, None]
        )
        pulled = jnp.einsum("gak,ck->gca", weighted, centre, precision=highest)
        return pieces[0] * jnp.sum(weighted, 2)[:, None, :] - pulled

    pushes = lax.map(force_pass, (coords_block, alive_blocks)).reshape(
        domains, capacity, 3, tile_len
    )
    returned = lax.all_to_all(pushes, "dom", split_axis=0, concat_axis=0, tiled=True)
    forces = jnp.einsum(
        "sn,sck->nck", matrix, returned.reshape(slot_total, 3, tile_len), precision=highest
    )
    return (forces, model_map)


def local(
    positions,
    velocities,
    charge,
    inverse_mass,
    pair_tiles,
    halo_tiles,
    owners,
    centres,
    widths,
    map_density,
    map_error,
    partner,
    decision,
):
    tile_count = pair_tiles.shape[0]
    tile_len = positions.shape[2] // tile_count
    position = positions[0].reshape(3, tile_count, tile_len).transpose(1, 0, 2)
    velocity = velocities[0].reshape(3, tile_count, tile_len).transpose(1, 0, 2)
    charges = charge.reshape(tile_count, tile_len)
    inverse = inverse_mass.reshape(tile_count, tile_len)
    intersection_scale = 1.0 / (owners.shape[1] * tile_count * tile_len)
    model_map = jnp.zeros_like(widths)
    for step_index in range(STEPS):
        pushed = nonbonded(position, charges, halo_tiles, pair_tiles)
        pulled, model_map = map_send(
            position, owners, centres, widths, map_density, map_error, intersection_scale
        )
        velocity = velocity + time_step * inverse[:, None, :] * (pushed + pulled)
        position = position + time_step * velocity
    replicas = lax.axis_size("rep")
    replica_ids = jnp.arange(replicas, dtype=jnp.int32)
    source = jnp.where(decision == 1, partner, replica_ids)
    my_source = jnp.sum(jnp.where(replica_ids == lax.axis_index("rep"), source, 0))
    pieces = (
        lax.all_gather(position[None], "rep", axis=0, tiled=True),
        lax.all_gather(velocity[None], "rep", axis=0, tiled=True),
    )
    row_ids = jnp.arange(pieces[0].shape[0], dtype=jnp.int32)
    matched = (row_ids == my_source).astype(jnp.float32)[:, None, None, None]
    position = jnp.sum(pieces[0] * matched, 0)
    velocity = jnp.sum(pieces[1] * matched, 0)
    new_positions = position.transpose(1, 0, 2).reshape(1, 3, tile_count * tile_len)
    new_velocities = velocity.transpose(1, 0, 2).reshape(1, 3, tile_count * tile_len)
    return (new_positions, new_velocities, model_map)


def solution(mesh):
    placed = (
        P("rep", None, "dom"),
        P("rep", None, "dom"),
        P("dom"),
        P("dom"),
        P("dom", None),
        P("dom", None, None),
        P("dom", None),
        P(None, "dom"),
        P("dom"),
        P("dom"),
        P("dom"),
        P(),
        P(),
    )
    return jax.shard_map(
        local,
        mesh=mesh,
        in_specs=placed,
        out_specs=(P("rep", None, "dom"), P("rep", None, "dom"), P("dom")),
        check_vma=False,
    )
```

profile of v0, /device:TPU:2, one launch (start us, length us, event | category | flops | bytes accessed | tf_op | source)
XLA Modules:
  0.0 410.8 jit_solution(8934856958367420256)
XLA Ops:
  2.8 15.5 %all-to-all-start.1 = ((f32[32,1,2]{2,1,0:T(1,128)}), f32[32,1,2]{2,1,0:T(1,128)S(1)}, u32[]{:S(2)}, u32[]{:S(2)}) async-start(f32[32,1,2]{2,1,0:T(1,128)} %bitcast.91), calls=%async_computation.1 | async-start | bytes 32768 | tf_op jit(solution)/shard_map/all_to_all | solution.py:117
  23.5 7.3 %all-to-all-done.1 = f32[32,1,2]{2,1,0:T(1,128)S(1)} async-done(((f32[32,1,2]{2,1,0:T(1,128)}), f32[32,1,2]{2,1,0:T(1,128)S(1)}, u32[]{:S(2)}, u32[]{:S(2)}) %all-to-all-start.1) | async-done | bytes 288 | tf_op jit(solution)/shard_map/all_to_all | solution.py:117
  30.7 4.9 %all-to-all-start = ((f32[32,2,3,128]{3,1,2,0:T(2,128)}), f32[32,2,3,128]{3,1,2,0:T(2,128)S(1)}, u32[]{:S(2)}, u32[]{:S(2)}) async-start(f32[32,2,3,128]{3,1,2,0:T(2,128)} %copy.219), calls=%async_computation | async-start | bytes 196608 | tf_op jit(solution)/shard_map/all_to_all | solution.py:116
  38.6 12.9 %all-to-all-done = f32[32,2,3,128]{3,1,2,0:T(2,128)S(1)} async-done(((f32[32,2,3,128]{3,1,2,0:T(2,128)}), f32[32,2,3,128]{3,1,2,0:T(2,128)S(1)}, u32[]{:S(2)}, u32[]{:S(2)}) %all-to-all-start) | async-done | bytes 98336 | tf_op jit(solution)/shard_map/all_to_all | solution.py:116
  51.6 20.1 %while.61 = (s32[]{:T(128)}, f32[16,1024]{1,0:T(8,128)S(1)}, f32[16,4,3,128]{3,1,0,2:T(4,128)S(1)}, f32[3,1024]{1,0:T(4,128)S(1)}, f32[1024]{0:T(1024)S(1)}, /*index=5*/f32[16,4]{1,0:T(8,128)S(1)}, s32[]{:T(128)}, s32[]{:T(128)}) while((s32[]{:T(128)}, f32[16,1024]{1,0:T(8,128)S(1)}, f32[16,4,3,128]{3,1,0,2:T(4,128)S(1)}, ...), condition=%wide.region_9.10_spmd, body=%wide.region_7.9_spmd.sunk | while | flops 6291458 | bytes 92305 | solution.py:128
  71.7 36.7 %psum.14 = f32[1024]{0:T(1024)S(1)} all-reduce(f32[1024]{0:T(1024)S(1)} %broadcast_multiply_fusion.6), channel_id=1, replica_groups=mesh['rep'=16,'dom'=32] {'rep'}, use_global_device_ids=true, to_apply=%region_11.12 | all-reduce | flops 1024 | bytes 8192 | tf_op jit(solution)/shard_map/psum | solution.py:130
  108.4 67.6 %while.62 = (s32[]{:T(128)}, f32[16,4,3,128]{3,2,1,0:T(4,128)S(1)}, f32[16,4,3,128]{3,1,0,2:T(4,128)S(1)}, f32[3,1024]{1,0:T(4,128)S(1)}, f32[1024]{0:T(1024)S(1...) while((s32[]{:T(128)}, f32[16,4,3,128]{3,2,1,0:T(4,128)S(1)}, ...), condition=%wide.region_14.15_spmd, body=%wide.region_12.14_spmd.sunk | while | flops 31985152 | bytes 158353 | solution.py:143
  122.5 2.9 fusion.141
  126.7 2.9 fusion.141
  130.9 2.9 fusion.141
  176.7 3.8 all-to-all-start.2
  180.6 6.1 %while.60 = (s32[]{:T(128)}, f32[2,4,3,128]{3,1,0,2:T(4,128)S(1)}, f32[2,4,4,128]{3,2,1,0:T(4,128)S(1)}, f32[2,4,6,4,128]{4,1,0,3,2:T(4,128)S(1)}, s32[]{:T(128)}) while((s32[]{:T(128)}, f32[2,4,3,128]{3,1,0,2:T(4,128)S(1)}, f32[2,4,4,128]{3,2,1,0:T(4,128)S(1)}, f32[2,4,6,4,128]{4,1,0,3,2:T(4,128)S(1)}, s32[]{:T(128)}) %tuple.217), condition=%wide.region_2.3_spmd, body=%wide.region_0.2_spmd.sunk | while | flops 23204352 | bytes 716873 | solution.py:101
  186.7 9.6 %all-to-all-done.2 = f32[32,2,3,128]{3,1,2,0:T(2,128)S(1)} async-done(((f32[32,2,3,128]{3,1,2,0:T(2,128)}), f32[32,2,3,128]{3,1,2,0:T(2,128)S(1)}, u32[]{:S(2)}, u32[]{:S(2)}) %all-to-all-start.2) | async-done | bytes 98336 | tf_op jit(solution)/shard_map/all_to_all | solution.py:146
  197.9 4.0 all-to-all-start.3
  202.0 2.9 collective-permute-start.3
  206.7 10.9 %all-to-all-done.3 = f32[32,2,3,128]{3,1,2,0:T(2,128)S(1)} async-done(((f32[32,2,3,128]{3,1,2,0:T(2,128)}), f32[32,2,3,128]{3,1,2,0:T(2,128)S(1)}, u32[]{:S(2)}, u32[]{:S(2)}) %all-to-all-start.3) | async-done | bytes 98336 | tf_op jit(solution)/shard_map/all_to_all | solution.py:116
  217.6 20.1 %while.64 = (s32[]{:T(128)}, f32[16,1024]{1,0:T(8,128)S(1)}, f32[16,4,3,128]{3,1,0,2:T(4,128)S(1)}, f32[3,1024]{1,0:T(4,128)S(1)}, f32[1024]{0:T(1024)S(1)}, /*index=5*/f32[16,4]{1,0:T(8,128)S(1)}, s32[]{:T(128)}, s32[]{:T(128)}) while((s32[]{:T(128)}, f32[16,1024]{1,0:T(8,128)S(1)}, f32[16,4,3,128]{3,1,0,2:T(4,128)S(1)}, ...), condition=%wide.region_20.21_spmd, body=%wide.region_18.20_spmd.sunk | while | flops 6291458 | bytes 92305 | solution.py:128
  237.7 40.0 %psum.15 = f32[1024]{0:T(1024)S(1)} all-reduce(f32[1024]{0:T(1024)S(1)} %broadcast_multiply_fusion.5), channel_id=1, replica_groups=mesh['rep'=16,'dom'=32] {'rep'}, use_global_device_ids=true, to_apply=%region_22.23 | all-reduce | flops 1024 | bytes 8192 | tf_op jit(solution)/shard_map/psum | solution.py:130
  278.3 67.6 %while.65 = (s32[]{:T(128)}, f32[16,4,3,128]{3,2,1,0:T(4,128)S(1)}, f32[16,4,3,128]{3,1,0,2:T(4,128)S(1)}, f32[3,1024]{1,0:T(4,128)S(1)}, f32[1024]{0:T(1024)S(1...) while((s32[]{:T(128)}, f32[16,4,3,128]{3,2,1,0:T(4,128)S(1)}, ...), condition=%wide.region_25.26_spmd, body=%wide.region_23.25_spmd.sunk | while | flops 31985152 | bytes 158353 | solution.py:143
  346.6 3.8 all-to-all-start.4
  350.5 6.1 %while.63 = (s32[]{:T(128)}, f32[2,4,3,128]{3,1,0,2:T(4,128)S(1)}, f32[2,4,4,128]{3,2,1,0:T(4,128)S(1)}, f32[2,4,6,4,128]{4,1,0,3,2:T(4,128)S(1)}, s32[]{:T(128)}) while((s32[]{:T(128)}, f32[2,4,3,128]{3,1,0,2:T(4,128)S(1)}, f32[2,4,4,128]{3,2,1,0:T(4,128)S(1)}, f32[2,4,6,4,128]{4,1,0,3,2:T(4,128)S(1)}, s32[]{:T(128)}) %tuple.216), condition=%wide.region_17.18_spmd, body=%wide.region_15.17_spmd.sunk | while | flops 23204352 | bytes 716873 | solution.py:101
  356.6 9.6 %all-to-all-done.4 = f32[32,2,3,128]{3,1,2,0:T(2,128)S(1)} async-done(((f32[32,2,3,128]{3,1,2,0:T(2,128)}), f32[32,2,3,128]{3,1,2,0:T(2,128)S(1)}, u32[]{:S(2)}, u32[]{:S(2)}) %all-to-all-start.4) | async-done | bytes 98336 | tf_op jit(solution)/shard_map/all_to_all | solution.py:146
  366.4 20.9 %all-gather = f32[128,3,128]{2,0,1:T(8,128)S(1)} all-gather(f32[8,3,128]{2,0,1:T(8,128)S(1)} %get-tuple-element.497), channel_id=2, replica_groups=mesh['rep'=16,'dom'=32] {'rep'}, dimensions={0}, use_global_device_ids=true | all-gather | bytes 208896 | tf_op jit(solution)/shard_map/all_gather | solution.py:188
  387.3 22.8 %all-gather.1 = f32[128,3,128]{2,0,1:T(8,128)S(1)} all-gather(f32[8,3,128]{2,0,1:T(8,128)S(1)} %get-tuple-element.498), channel_id=3, replica_groups=mesh['rep'=16,'dom'=32] {'rep'}, dimensions={0}, use_global_device_ids=true | all-gather | bytes 208896 | tf_op jit(solution)/shard_map/all_gather | solution.py:189
  (618 shorter events, 191.3 us)
Async XLA Ops:
  0.6 21.8 %copy-start.2 = (f32[1,3,1024]{2,0,1:T(1,128)S(1)}, f32[1,3,1024]{2,0,1:T(1,128)}, u32[]{:S(2)}) copy-start(f32[1,3,1024]{2,0,1:T(1,128)} %param.25) | copy-start | bytes 36868
  0.6 21.7 %copy-start.7 = (f32[1024]{0:T(1024)S(1)}, f32[1024]{0:T(1024)}, u32[]{:S(2)}) copy-start(f32[1024]{0:T(1024)} %param.28) | copy-start | bytes 12292
  2.0 20.7 %copy-start.3 = (f32[1024]{0:T(1024)S(1)}, f32[1024]{0:T(1024)}, u32[]{:S(2)}) copy-start(f32[1024]{0:T(1024)} %param.27) | copy-start | bytes 12292
  2.8 27.9 %all-to-all-start.1 = ((f32[32,1,2]{2,1,0:T(1,128)}), f32[32,1,2]{2,1,0:T(1,128)S(1)}, u32[]{:S(2)}, u32[]{:S(2)}) async-start(f32[32,1,2]{2,1,0:T(1,128)} %bitcast.91), calls=%async_computation.1 | async-start | bytes 32768 | tf_op jit(solution)/shard_map/all_to_all | solution.py:117
  19.3 19.1 %collective-permute-start = (f32[1,2,4,128]{3,1,2,0:T(2,128)S(1)}, f32[1,2,4,128]{3,1,2,0:T(2,128)S(1)}, u32[]{:S(2)}, u32[]{:S(2)}) collective-permute-start(f32[1,2,4,128]{3,1,2,0:T(2,128)S(1)} %get-tuple-element.493), channel_id=1, source_target_pairs={{0,1},{1,2},{2,3},{3,4},{4,5},{5,6},{6,7},{7,8},{8,9},{9,10},{10,1... | collective-permute-start | bytes 12296 | tf_op jit(solution)/shard_map/ppermute | solution.py:21
  19.5 18.8 %collective-permute-start.1 = (f32[1,2,4,128]{3,1,2,0:T(2,128)S(1)}, f32[1,2,4,128]{3,1,2,0:T(2,128)S(1)}, u32[]{:S(2)}, u32[]{:S(2)}) collective-permute-start(f32[1,2,4,128]{3,1,2,0:T(2,128)S(1)} %get-tuple-element.494), channel_id=1, source_target_pairs={{1,0},{2,1},{3,2},{4,3},{5,4},{6,5},{7,6},{8,7},{9,8},{10,9},{11,1... | collective-permute-start | bytes 12296 | tf_op jit(solution)/shard_map/ppermute | solution.py:24
  22.7 12.9 %copy-start.9 = (s32[16]{0:T(128)S(1)}, s32[16]{0:T(128)}, u32[]{:S(2)}) copy-start(s32[16]{0:T(128)} %param.36) | copy-start | bytes 196
  22.8 12.9 %copy-start.10 = (s32[16]{0:T(128)S(1)}, s32[16]{0:T(128)}, u32[]{:S(2)}) copy-start(s32[16]{0:T(128)} %param.37) | copy-start | bytes 196
  22.8 14.2 %copy-start.8 = (s32[8,6]{1,0:T(8,128)S(1)}, s32[8,6]{1,0:T(8,128)}, u32[]{:S(2)}) copy-start(s32[8,6]{1,0:T(8,128)} %param.29) | copy-start | bytes 580
  30.7 20.8 %all-to-all-start = ((f32[32,2,3,128]{3,1,2,0:T(2,128)}), f32[32,2,3,128]{3,1,2,0:T(2,128)S(1)}, u32[]{:S(2)}, u32[]{:S(2)}) async-start(f32[32,2,3,128]{3,1,2,0:T(2,128)} %copy.219), calls=%async_computation | async-start | bytes 196608 | tf_op jit(solution)/shard_map/all_to_all | solution.py:116
  38.4 13.2 %copy-start = (f32[3,1024]{1,0:T(4,128)S(1)}, f32[3,1024]{1,0:T(4,128)}, u32[]{:S(2)}) copy-start(f32[3,1024]{1,0:T(4,128)} %param.32) | copy-start | bytes 36868
  38.4 13.2 %copy-start.1 = (f32[1024]{0:T(1024)S(1)}, f32[1024]{0:T(1024)}, u32[]{:S(2)}) copy-start(f32[1024]{0:T(1024)} %param.33) | copy-start | bytes 12292
  51.6 56.8 %copy-start.4 = (f32[1024]{0:T(1024)S(1)}, f32[1024]{0:T(1024)}, u32[]{:S(2)}) copy-start(f32[1024]{0:T(1024)} %param.34) | copy-start | bytes 12292
  51.6 56.8 %copy-start.5 = (f32[1024]{0:T(1024)S(1)}, f32[1024]{0:T(1024)}, u32[]{:S(2)}) copy-start(f32[1024]{0:T(1024)} %param.35) | copy-start | bytes 12292
  176.7 19.6 %all-to-all-start.2 = ((f32[32,2,3,128]{3,1,2,0:T(2,128)}), f32[32,2,3,128]{3,1,2,0:T(2,128)S(1)}, u32[]{:S(2)}, u32[]{:S(2)}) async-start(f32[32,2,3,128]{3,1,2,0:T(2,128)} %copy.225), calls=%async_computation.2 | async-start | bytes 196608 | tf_op jit(solution)/shard_map/all_to_all | solution.py:146
  186.7 9.7 %copy-start.6 = (f32[1,3,1024]{2,0,1:T(1,128)S(1)}, f32[1,3,1024]{2,0,1:T(1,128)}, u32[]{:S(2)}) copy-start(f32[1,3,1024]{2,0,1:T(1,128)} %param.26) | copy-start | bytes 36868
  196.3 0.7 copy-start.11
  197.9 19.6 %all-to-all-start.3 = ((f32[32,2,3,128]{3,1,2,0:T(2,128)}), f32[32,2,3,128]{3,1,2,0:T(2,128)S(1)}, u32[]{:S(2)}, u32[]{:S(2)}) async-start(f32[32,2,3,128]{3,1,2,0:T(2,128)} %copy.231), calls=%async_computation.3 | async-start | bytes 196608 | tf_op jit(solution)/shard_map/all_to_all | solution.py:116
  202.0 4.5 %collective-permute-start.2 = (f32[1,2,4,128]{3,1,2,0:T(2,128)S(1)}, f32[1,2,4,128]{3,1,2,0:T(2,128)S(1)}, u32[]{:S(2)}, u32[]{:S(2)}) collective-permute-start(f32[1,2,4,128]{3,1,2,0:T(2,128)S(1)} %get-tuple-element.491), channel_id=1, source_target_pairs={{0,1},{1,2},{2,3},{3,4},{4,5},{5,6},{6,7},{7,8},{8,9},{9,10},{10,1... | collective-permute-start | bytes 12296 | tf_op jit(solution)/shard_map/ppermute | solution.py:21
  202.0 4.5 %collective-permute-start.3 = (f32[1,2,4,128]{3,1,2,0:T(2,128)S(1)}, f32[1,2,4,128]{3,1,2,0:T(2,128)S(1)}, u32[]{:S(2)}, u32[]{:S(2)}) collective-permute-start(f32[1,2,4,128]{3,1,2,0:T(2,128)S(1)} %get-tuple-element.492), channel_id=1, source_target_pairs={{1,0},{2,1},{3,2},{4,3},{5,4},{6,5},{7,6},{8,7},{9,8},{10,9},{11,1... | collective-permute-start | bytes 12296 | tf_op jit(solution)/shard_map/ppermute | solution.py:24
  346.6 19.6 %all-to-all-start.4 = ((f32[32,2,3,128]{3,1,2,0:T(2,128)}), f32[32,2,3,128]{3,1,2,0:T(2,128)S(1)}, u32[]{:S(2)}, u32[]{:S(2)}) async-start(f32[32,2,3,128]{3,1,2,0:T(2,128)} %copy.236), calls=%async_computation.4 | async-start | bytes 196608 | tf_op jit(solution)/shard_map/all_to_all | solution.py:146
where the time goes:
time: 412 us; the launch traced here: 411 us
  blocking collectives  120 us (29%)
  matrix products  103 us (25%)
  other arithmetic  80.3 us (19%)
  waiting for transfers between devices  51.7 us (13%)
  starting transfers between devices  38 us (9%)
  local copies, waits for them, and re-layouts  12.3 us (3%)
  loops' own time  4.2 us (1%)
    dot_general x32, matrix products, force_pass(): pulled = jnp.einsum('gak,ck->gca', weighted, centre, precision=highest)  92.4 us
    psum x2, blocking collectives, map_send(): totals = lax.psum(partial_value, 'rep')  76.7 us
    reduce_sum x32, other arithmetic, force_pass(): return pieces[0] * jnp.sum(weighted, 2)[:, None, :] - pulled  39.7 us
    reduce_sum x32, other arithmetic, intersection_pass(): jnp.sum(slot_gaussians(pieces[0], centre, extent) * pieces[1][:, None, No...  33.2 us
    all_to_all x2, waiting for transfers between devices, map_send(): lax.all_to_all(outgoing, 'dom', split_axis=0, concat_axis=0, tiled=True)  23.7 us
    all_gather x1, blocking collectives, local(): lax.all_gather(velocity[None], 'rep', axis=0, tiled=True)  22.8 us
    all_gather x1, blocking collectives, local(): lax.all_gather(position[None], 'rep', axis=0, tiled=True)  20.9 us
    all_to_all x2, waiting for transfers between devices, map_send(): lax.all_to_all(pushes, 'dom', split_axis=0, concat_axis=0, tiled=True)  19.2 us
  transfers between devices with their start and end apart: 9, of which 6 were waited for; matrix products, arithmetic and copies ran while one was open for 4% of the time, Pallas kernels for 0%

commit v1 on v0

v1 whole, which is shorter than its diff:
```python
import functools
import math

import jax
import jax.numpy as jnp
from jax import lax
from jax.experimental import pallas as pl
from jax.experimental.pallas import tpu as pltpu
from jax.sharding import PartitionSpec as P

STEPS = 2
TIME_STEP = 0.5
MAP_SCALE = 2.0
LOG2E = 1.4426950408889634
F32 = jnp.float32
BF16 = jnp.bfloat16
MESH = pl.DeviceIdType.MESH
NN = (((1,), (0,)), ((), ()))
NT = (((1,), (1,)), ((), ()))
LANES = 128
GROUPS = 8


def dot(a, b, dims):
    return lax.dot_general(a, b, dims, preferred_element_type=F32)


def split3(v):
    h = v.astype(BF16).astype(F32)
    rest = v - h
    m = rest.astype(BF16).astype(F32)
    return h, m, rest - m


def kernel(
    reps, doms, near, owned,
    pos, vel, charge, imass, pair, halo, owners, inv, cen, wid, den, err, partner, decision,
    opos, ovel, omap,
    row, out2, col, own, hs, hr, raw, pa, cf, ad, bf, qf, scr, scr2, at, pb, pq, fp, g2, part,
    d1, r1, t1, r2, cs, co, ms, mm,
    sem_px, sem_py, sem_a, sem_ad, sem_b, sem_c, sem_h, sem_hs, sem_1, sem_2, sem_3, sem_m,
):
    width = math.isqrt(reps)
    height = reps // width
    levels = doms // 2
    classes = reps // 4
    held = levels // classes
    tiles = 8
    slots = tiles * owned
    plane = 2 * reps

    r = lax.axis_index("rep")
    dom = lax.axis_index("dom")
    z = lax.div(dom, 2)
    c = lax.rem(dom, 2)
    y = lax.div(r, width)
    x = lax.rem(r, width)
    p = 2 * r + c
    below = lax.rem(dom + doms - 1, doms)
    above = lax.rem(dom + 1, doms)

    def plane_peer(i):
        k = lax.rem(p + i, plane)
        return k, (lax.div(k, 2), 2 * z + lax.rem(k, 2))

    def level_peer(i):
        return (r, 2 * lax.rem(z + i, levels) + c)

    def rep_peer(i):
        return (lax.rem(r + i, reps), dom)

    other_core = (r, 2 * z + 1 - c)

    def send(src, dst, sems, to):
        pltpu.make_async_remote_copy(
            src_ref=src, dst_ref=dst, send_sem=sems.at[0], recv_sem=sems.at[1],
            device_id=to, device_id_type=MESH,
        ).start()

    def each(count, body):
        def step(i, carry):
            body(i)
            return carry

        lax.fori_loop(1, count, step, 0)

    def received(ref, sems):
        pltpu.make_async_copy(ref, ref, sems.at[1]).wait()

    def sent(ref, sems):
        pltpu.make_async_copy(ref, ref, sems.at[0]).wait()

    barrier = pltpu.get_barrier_semaphore()

    def greet(to):
        pl.semaphore_signal(barrier, inc=1, device_id=to, device_id_type=MESH)

    each(plane, lambda i: greet(plane_peer(i)[1]))
    each(levels, lambda i: greet(level_peer(i)))
    greet((r, jnp.where(c == 0, below, above)))

    for t in range(tiles):
        for k in range(3):
            cut = slice(t * LANES, (t + 1) * LANES)
            row[x, k, t : t + 1, :] = pos[0, k : k + 1, cut]
            row[x, 3 + k, t : t + 1, :] = vel[0, k : k + 1, cut]
    for k in range(3):
        for g in range(GROUPS):
            raw[k, g : g + 1, :] = cen[k : k + 1, g * LANES : (g + 1) * LANES]
    raw[3] = wid[...]
    scr[...] = jnp.zeros_like(scr)
    scr2[...] = jnp.zeros_like(scr2)
    part[slots] = jnp.zeros((GROUPS, LANES), F32)

    pl.semaphore_wait(barrier, plane - 1 + levels - 1 + 1)

    each(width, lambda i: send(row.at[x], row.at[x], sem_px, (y * width + lax.rem(x + i, width), dom)))

    feature = lax.rem(r, 4)
    sender = lax.rem(z, classes) == lax.div(r, 4)
    place = lax.div(z, classes)

    @pl.when(sender)
    def _():
        each(levels, lambda i: send(raw.at[feature], pa.at[place], sem_a, level_peer(i)))
        pa[place] = raw[feature]

    @pl.when(z == r)
    def _():
        error = err[...]
        ad[0] = (MAP_SCALE / (owned * GROUPS * LANES)) / (error * error) / wid[...]
        ad[1] = den[...]
        each(levels, lambda i: send(ad, ad, sem_ad, level_peer(i)))

    if held > 1:
        @pl.when(sender)
        def _():
            received(pa.at[pl.ds(0, held - 1)], sem_a)

    @pl.when(jnp.logical_not(sender))
    def _():
        received(pa, sem_a)

    each(reps, lambda i: send(pa, cf.at[c, r], sem_b, rep_peer(i)))
    cf[c, r] = pa[...]

    def source_of(k):
        return jnp.where(decision[k] == 1, partner[k], k)

    received(row.at[pl.ds(0, width - 1)], sem_px)
    for i in range(1, height):
        there = lax.rem(y + i, height)
        to = there * width + x
        out2[i - 1] = row[lax.rem(source_of(to), width)]
        send(out2.at[i - 1], col.at[y], sem_py, (to, dom))
    mine = source_of(r)
    col[y] = row[lax.rem(mine, width)]
    received(col.at[pl.ds(0, height - 1)], sem_py)
    state = col[lax.div(mine, width)]
    for t in range(tiles):
        for k in range(3):
            own[t, k : k + 1, :] = state[k, t : t + 1, :]
            own[t, 4 + k : 5 + k, :] = state[3 + k, t : t + 1, :]
        own[t, 3:4, :] = charge[t : t + 1, :]
        own[t, 7:8, :] = imass[t : t + 1, :]

    def send_halo(s):
        for side, to in ((0, below), (1, above)):
            for i in range(2):
                hs[s, side, i] = own[halo[0, side, i]]
            pltpu.make_async_remote_copy(
                src_ref=hs.at[s, side], dst_ref=hr.at[s, 1 - side],
                send_sem=sem_hs.at[s, side], recv_sem=sem_h.at[s, side],
                device_id=(r, to), device_id_type=MESH,
            ).start()

    def wait_halo(s):
        for side in range(2):
            pltpu.make_async_copy(hr.at[s, 1 - side], hr.at[s, 1 - side], sem_h.at[s, side]).wait()

    send_halo(0)

    def basis(zz, cc):
        cut = lax.div(zz, classes)
        base = lax.rem(zz, classes) * 4
        cx, cy, cz, w = (cf[cc, base + f, cut] for f in range(4))
        return cx, cy, cz, w

    def component_features(cc):
        def step(zz, carry):
            cx, cy, cz, w = basis(zz, cc)
            iw = LOG2E / w
            half = -0.5 * iw
            terms = [split3(v) for v in (cx * iw, cy * iw, cz * iw, half)]
            for group, level in enumerate((0, 1, 0, 2, 0, 1)):
                for f in range(4):
                    scr[pl.ds(group * 4 + f, GROUPS, stride=32), :] = terms[f][level]
            for level, v in enumerate(split3(half * (cx * cx + cy * cy + cz * cz))):
                scr[pl.ds(24 + level, GROUPS, stride=32), :] = v
            o = 2 * zz + cc
            for g in range(GROUPS):
                bf[o, :, g * LANES : (g + 1) * LANES] = scr[g * 32 : (g + 1) * 32, :].astype(BF16)
            return carry

        lax.fori_loop(0, levels, step, 0)

    def coefficient_features(s):
        def one(zz, cc):
            cx, cy, cz, _ = basis(zz, cc)
            o = 2 * zz + cc
            coef = co[s, o]
            for f, v in enumerate((coef, coef * cx, coef * cy, coef * cz)):
                for level, piece in enumerate(split3(v)):
                    scr2[pl.ds(level * 4 + f, GROUPS, stride=16), :] = piece
            for g in range(GROUPS):
                qf[o, :, g * LANES : (g + 1) * LANES] = scr2[g * 16 : (g + 1) * 16, :].astype(BF16)

        def step(zz, carry):
            one(zz, 0)
            one(zz, 1)
            return carry

        lax.fori_loop(0, levels, step, 0)

    ones3 = jnp.ones((3, LANES), F32)
    zeros4 = jnp.zeros((4, LANES), F32)
    zeros5 = jnp.zeros((5, LANES), F32)

    def atom_features():
        for t in range(tiles):
            xyz = own[t, 0:3, :]
            h, m, l = split3(jnp.concatenate([xyz, jnp.sum(xyz * xyz, 0, keepdims=True)], 0))
            rows = jnp.concatenate([h, h, m, h, l, m, ones3, zeros5], 0)
            at[t] = rows.T.astype(BF16)

    def pair_features(s):
        for i in range(tiles + 4):
            tile = own[i] if i < tiles else hr[s, (i - tiles) // 2, (i - tiles) % 2]
            xyz = tile[0:3]
            h, m, l = split3(jnp.concatenate([xyz * LOG2E, jnp.full((1, LANES), -0.5 * LOG2E, F32)], 0))
            ch, cm, cl = split3((-0.5 * LOG2E) * jnp.sum(xyz * xyz, 0, keepdims=True))
            pb[i] = jnp.concatenate([h, m, h, l, h, m, ch, cm, cl, zeros5], 0).astype(BF16)
            q = tile[3:4]
            h, m, l = split3(jnp.concatenate([q, q * xyz], 0))
            pq[i] = jnp.concatenate([h, m, l, zeros4], 0).astype(BF16)
        pb[tiles + 4] = jnp.zeros((32, LANES), BF16)
        pq[tiles + 4] = jnp.zeros((16, LANES), BF16)

    def halves(g):
        h = g.astype(BF16)
        return h, (g - h.astype(F32)).astype(BF16)

    def pulled(sums, xyz):
        sums = sums[0:4] + sums[4:8] + sums[8:12]
        return xyz * sums[0:1] - sums[1:4]

    pair_gain = (near * LANES) ** -0.5

    def pair_pass():
        def step(t, carry):
            names = [pair[t, j] for j in range(near)]
            names = [jnp.where(n < 0, tiles + 4, n) for n in names]
            g = jnp.exp2(dot(at[t], jnp.concatenate([pb[n] for n in names], 1), NN))
            q = jnp.concatenate([pq[n] for n in names], 1)
            h, l = halves(g)
            sums = dot(q, h, NT) + dot(q, l, NT)
            fp[t, 0:3, :] = (pair_gain * own[t, 3:4, :]) * pulled(sums, own[t, 0:3, :])
            return carry

        lax.fori_loop(0, tiles, step, 0)

    chunk = 256

    def intersection_pass():
        def step(t, carry):
            a = at[t]
            for j in range(owned):
                o = owners[t, j]
                n = t * owned + j
                for q in range(GROUPS * LANES // chunk):
                    cut = slice(q * chunk, (q + 1) * chunk)
                    g = jnp.exp2(dot(a, bf[o, :, cut], NN))
                    total = jnp.sum(g, 0, keepdims=True)
                    for i in range(chunk // LANES):
                        k = q * (chunk // LANES) + i
                        part[n, k : k + 1, :] = total[:, i * LANES : (i + 1) * LANES]
                    h, l = halves(g)
                    g2[n, 0:LANES, cut] = h
                    g2[n, LANES : 2 * LANES, cut] = l
            return carry

        lax.fori_loop(0, tiles, step, 0)

    def force_pass():
        def step(t, carry):
            sums = jnp.zeros((16, 2 * LANES), F32)
            for j in range(owned):
                sums = sums + dot(qf[owners[t, j]], g2[t * owned + j], NT)
            sums = sums[:, :LANES] + sums[:, LANES:]
            xyz = own[t, 0:3, :]
            force = fp[t, 0:3, :] + pulled(sums, xyz)
            v = own[t, 4:7, :] + TIME_STEP * own[t, 7:8, :] * force
            own[t, 4:7, :] = v
            own[t, 0:3, :] = xyz + TIME_STEP * v
            return carry

        lax.fori_loop(0, tiles, step, 0)

    received(cf.at[c, pl.ds(0, reps - 1)], sem_b)
    send(cf.at[c], cf.at[c], sem_c, other_core)
    atom_features()
    component_features(c)
    received(cf.at[1 - c], sem_c)
    component_features(1 - c)

    @pl.when(z != r)
    def _():
        received(ad, sem_ad)

    for s in range(STEPS):
        if s > 0:
            send_halo(s)
            atom_features()
        intersection_pass()

        def gather(k, carry, s=s):
            d1[s, k] = part[inv[0, k]] + part[inv[1, k]]
            return carry

        lax.fori_loop(0, plane, gather, 0)

        def scatter(i, s=s):
            k, to = plane_peer(i)
            send(d1.at[s, k], r1.at[s, p], sem_1.at[s], to)

        each(plane, scatter)
        r1[s, p] = d1[s, p]

        wait_halo(s)
        pair_features(s)
        pair_pass()

        received(r1.at[s, pl.ds(0, plane - 1)], sem_1.at[s])
        total = jnp.sum(r1[s], 0)
        t1[s] = total
        each(levels, lambda i, s=s: send(t1.at[s], r2.at[s, z], sem_2.at[s], level_peer(i)))
        r2[s, z] = total
        received(r2.at[s, pl.ds(0, levels - 1)], sem_2.at[s])
        mean = jnp.sum(r2[s], 0) * (1.0 / (owned * tiles * LANES * reps))
        coef = ad[0] * (mean - ad[1])
        cs[s] = coef
        each(plane, lambda i, s=s: send(cs.at[s], co.at[s, p], sem_3.at[s], plane_peer(i)[1]))
        co[s, p] = coef
        if s == STEPS - 1:
            @pl.when(z == r)
            def _(mean=mean):
                ms[...] = mean
                omap[...] = mean
                each(reps, lambda i: send(ms, mm, sem_m, rep_peer(i)))

        received(co.at[s, pl.ds(0, plane - 1)], sem_3.at[s])
        coefficient_features(s)
        force_pass()

    for t in range(tiles):
        cut = slice(t * LANES, (t + 1) * LANES)
        opos[0, :, cut] = own[t, 0:3, :]
        ovel[0, :, cut] = own[t, 4:7, :]

    @pl.when(z != r)
    def _():
        received(mm, sem_m)
        omap[...] = mm[...]

    sent(row.at[pl.ds(0, width - 1)], sem_px)
    sent(out2, sem_py)

    @pl.when(sender)
    def _():
        sent(r2.at[0, pl.ds(0, levels - 1)], sem_a)

    @pl.when(z == r)
    def _():
        sent(d1.at[0, pl.ds(0, 2 * (levels - 1))], sem_ad)
        sent(d1.at[0, pl.ds(0, reps - 1)], sem_m)

    sent(cf.at[0, pl.ds(0, reps - 1)], sem_b)
    sent(cf.at[0], sem_c)
    for s in range(STEPS):
        for side in range(2):
            pltpu.make_async_copy(hs.at[s, side], hs.at[s, side], sem_hs.at[s, side]).wait()
        sent(d1.at[s, pl.ds(0, plane - 1)], sem_1.at[s])
        sent(r2.at[s, pl.ds(0, levels - 1)], sem_2.at[s])
        sent(co.at[s, pl.ds(0, plane - 1)], sem_3.at[s])


def local(
    positions, velocities, charge, inverse_mass, pair_tiles, halo_tiles, owners,
    centres, widths, map_density, map_error, partner, decision,
):
    reps = lax.axis_size("rep")
    doms = lax.axis_size("dom")
    tiles, near = pair_tiles.shape
    owned = owners.shape[1]
    slots = tiles * owned
    levels = doms // 2
    width = math.isqrt(reps)
    height = reps // width
    held = levels // (reps // 4)
    plane = 2 * reps

    named = owners.reshape(1, slots) == jnp.arange(doms, dtype=jnp.int32)[:, None]
    ids = jnp.arange(slots, dtype=jnp.int32)[None, :]
    first = jnp.min(jnp.where(named, ids, slots), 1)
    last = jnp.max(jnp.where(named, ids, -1), 1)
    inv = jnp.stack([first, jnp.where(last > first, last, slots)])

    def square(v):
        return v.reshape(GROUPS, LANES)

    tile = (GROUPS, LANES)
    vmem = pl.BlockSpec(memory_space=pltpu.VMEM)
    smem = pl.BlockSpec(memory_space=pltpu.SMEM)
    pair_sems = pltpu.SemaphoreType.DMA((2,))
    step_sems = pltpu.SemaphoreType.DMA((STEPS, 2))
    outs = pl.pallas_call(
        functools.partial(kernel, reps, doms, near, owned),
        out_shape=[
            jax.ShapeDtypeStruct(positions.shape, F32),
            jax.ShapeDtypeStruct(velocities.shape, F32),
            jax.ShapeDtypeStruct(tile, F32),
        ],
        in_specs=[vmem] * 4 + [smem] * 4 + [vmem] * 4 + [smem] * 2,
        out_specs=[vmem] * 3,
        scratch_shapes=[
            pltpu.VMEM((width, 6) + tile, F32),
            pltpu.VMEM((height - 1, 6) + tile, F32),
            pltpu.VMEM((height, 6) + tile, F32),
            pltpu.VMEM((tiles,) + tile, F32),
            pltpu.VMEM((STEPS, 2, 2) + tile, F32),
            pltpu.VMEM((STEPS, 2, 2) + tile, F32),
            pltpu.VMEM((4,) + tile, F32),
            pltpu.VMEM((held,) + tile, F32),
            pltpu.VMEM((2, reps, held) + tile, F32),
            pltpu.VMEM((2,) + tile, F32),
            pltpu.VMEM((doms, 32, GROUPS * LANES), BF16),
            pltpu.VMEM((doms, 16, GROUPS * LANES), BF16),
            pltpu.VMEM((GROUPS * 32, LANES), F32),
            pltpu.VMEM((GROUPS * 16, LANES), F32),
            pltpu.VMEM((tiles, LANES, 32), BF16),
            pltpu.VMEM((tiles + 5, 32, LANES), BF16),
            pltpu.VMEM((tiles + 5, 16, LANES), BF16),
            pltpu.VMEM((tiles,) + tile, F32),
            pltpu.VMEM((slots, 2 * LANES, GROUPS * LANES), BF16),
            pltpu.VMEM((slots + 1,) + tile, F32),
            pltpu.VMEM((STEPS, plane) + tile, F32),
            pltpu.VMEM((STEPS, plane) + tile, F32),
            pltpu.VMEM((STEPS,) + tile, F32),
            pltpu.VMEM((STEPS, levels) + tile, F32),
            pltpu.VMEM((STEPS,) + tile, F32),
            pltpu.VMEM((STEPS, plane) + tile, F32),
            pltpu.VMEM(tile, F32),
            pltpu.VMEM(tile, F32),
            pair_sems, pair_sems, pair_sems, pair_sems, pair_sems, pair_sems,
            step_sems, step_sems, step_sems, step_sems, step_sems,
            pair_sems,
        ],
        compiler_params=pltpu.CompilerParams(
            collective_id=0, has_side_effects=True, vmem_limit_bytes=44 * 1024 * 1024
        ),
    )(
        positions, velocities, square(charge), square(inverse_mass), pair_tiles, halo_tiles, owners,
        inv, centres, square(widths), square(map_density), square(map_error), partner, decision,
    )
    return outs[0], outs[1], outs[2].reshape(GROUPS * LANES)


def solution(mesh):
    placed = (
        P("rep", None, "dom"),
        P("rep", None, "dom"),
        P("dom"),
        P("dom"),
        P("dom", None),
        P("dom", None, None),
        P("dom", None),
        P(None, "dom"),
        P("dom"),
        P("dom"),
        P("dom"),
        P(),
        P(),
    )
    return jax.shard_map(
        local,
        mesh=mesh,
        in_specs=placed,
        out_specs=(P("rep", None, "dom"), P("rep", None, "dom"), P("dom")),
        check_vma=False,
    )
```

time: 412 us -> 99 us (0.24)
  the two profiles are of different devices: /device:TPU:2 before, /device:TPU:1 now
where the time goes in v1:
time: 99 us; the launch traced here: 98.8 us
  Pallas kernels  93.9 us (95%)
  local copies, waits for them, and re-layouts  3.97 us (4%)
    pallas_call x1, Pallas kernels, local(): pl.pallas_call(functools.partial(kernel, reps, doms, near, owned), out_sh...  93.9 us
    unnamed x32, local copies, waits for them, and re-layouts  3.89 us

profile of v1, /device:TPU:1, one launch (start us, length us, event | category | flops | bytes accessed | tf_op | source)
XLA Modules:
  0.0 98.8 jit_solution(10012831208921792505)
XLA Ops:
  0.6 0.0 copy-start.12
  0.6 0.0 copy-start.10
  0.6 0.7 copy-done.12
  1.3 0.1 copy.31.owners
  1.4 0.1 eq.15
  1.5 0.1 select_reduce_fusion.1
  1.6 0.0 copy-start.11
  1.6 0.0 copy-start.4
  1.7 0.0 copy-start.5
  1.7 0.0 copy-start.6
  1.7 0.0 copy-start.7
  1.7 0.0 copy-start.8
  1.7 0.0 copy-start.9
  1.7 0.6 copy-done.11
  2.4 0.0 copy-done.4
  2.4 0.0 copy-done.5
  2.4 0.0 copy-done.6
  2.4 0.0 copy-done.7
  2.4 0.6 copy-done
  3.1 0.0 copy-done.3
  3.1 93.9 %shard_map.148 = (f32[1,3,1024]{2,1,0:T(4,128)S(1)}, f32[1,3,1024]{2,1,0:T(4,128)S(1)}, f32[8,128]{1,0:T(8,128)S(1)}) custom-call(f32[1,3,1024]{2,1,0:T(4,128)S(1)} %copy.29.pos, f32[1,3,1024]{2,1,0:T(4,128)S(1)} %copy.30.vel, f32[8,128]{1,0:T(8,128)S(1)} %bitcast.10, f32[8,128]{1,0:T(8,128)S(1)} %bitcast.11, s32[8,6]{1,0:T(8,128)S(1)} %copy-done.3, ...), custom_call_target="tpu_custom_call" | custom-call | tf_op jit(solution)/shard_map/pallas_call | solution.py:426
  97.0 0.6 copy.32
  97.6 0.6 copy.33
  98.2 0.6 copy.35
  (13 shorter events, 0.0 us)
Async XLA Ops:
  0.6 0.7 copy-start.12
  0.6 1.0 copy-start.10
  1.6 0.7 copy-start.11
  1.6 0.7 copy-start.4
  1.7 0.7 copy-start.5
  1.7 0.7 copy-start.6
  1.7 0.7 copy-start.7
  1.7 0.7 copy-start.8
  1.7 0.7 copy-start.9
  2.3 0.7 copy-start
  2.3 0.7 copy-start.1
  2.3 0.7 copy-start.2
  2.4 0.7 copy-start.3

commit v2 on v1

--- a/solution.py
+++ b/solution.py
@@ -36,7 +36,7 @@
     reps, doms, near, owned,
     pos, vel, charge, imass, pair, halo, owners, inv, cen, wid, den, err, partner, decision,
     opos, ovel, omap,
-    row, out2, col, own, hs, hr, raw, pa, cf, ad, bf, qf, scr, scr2, at, pb, pq, fp, g2, part,
+    row, out2, col, own, hs, hr, raw, pa, cf, ad, bf, bt, qf, scr, scr2, at, ar, pb, pq, fp, g2, part,
     d1, r1, t1, r2, cs, co, ms, mm,
     sem_px, sem_py, sem_a, sem_ad, sem_b, sem_c, sem_h, sem_hs, sem_1, sem_2, sem_3, sem_m,
 ):
@@ -59,15 +59,25 @@
     below = lax.rem(dom + doms - 1, doms)
     above = lax.rem(dom + 1, doms)
 
-    def plane_peer(i):
-        k = lax.rem(p + i, plane)
-        return k, (lax.div(k, 2), 2 * z + lax.rem(k, 2))
+    def around(i, count):
+        return min(i, count - i)
+
+    def wrap(v, count):
+        return jnp.where(v >= count, v - count, v)
+
+    offsets = [(i, j, k) for i in range(height) for j in range(width) for k in range(2)]
+    offsets.sort(key=lambda o: -(around(o[0], height) + around(o[1], width) + 0.1 * o[2]))
+    plane_offsets = offsets[:-1]
+    rep_offsets = [o for o in plane_offsets if o[2] == 0]
+    level_offsets = sorted(range(1, levels), key=lambda i: -around(i, levels))
+
+    def plane_peer(o):
+        there = wrap(y + o[0], height) * width + wrap(x + o[1], width)
+        core = 1 - c if o[2] else c
+        return 2 * there + core, (there, 2 * z + core)
 
     def level_peer(i):
-        return (r, 2 * lax.rem(z + i, levels) + c)
-
-    def rep_peer(i):
-        return (lax.rem(r + i, reps), dom)
+        return (r, 2 * wrap(z + i, levels) + c)
 
     other_core = (r, 2 * z + 1 - c)
 
@@ -77,13 +87,6 @@
             device_id=to, device_id_type=MESH,
         ).start()
 
-    def each(count, body):
-        def step(i, carry):
-            body(i)
-            return carry
-
-        lax.fori_loop(1, count, step, 0)
-
     def received(ref, sems):
         pltpu.make_async_copy(ref, ref, sems.at[1]).wait()
 
@@ -95,15 +98,14 @@
     def greet(to):
         pl.semaphore_signal(barrier, inc=1, device_id=to, device_id_type=MESH)
 
-    each(plane, lambda i: greet(plane_peer(i)[1]))
-    each(levels, lambda i: greet(level_peer(i)))
+    for i in level_offsets:
+        greet(level_peer(i))
+    for o in plane_offsets:
+        greet(plane_peer(o)[1])
     greet((r, jnp.where(c == 0, below, above)))
 
-    for t in range(tiles):
-        for k in range(3):
-            cut = slice(t * LANES, (t + 1) * LANES)
-            row[x, k, t : t + 1, :] = pos[0, k : k + 1, cut]
-            row[x, 3 + k, t : t + 1, :] = vel[0, k : k + 1, cut]
+    row[x, 0:3] = pos[...]
+    row[x, 3:6] = vel[...]
     for k in range(3):
         for g in range(GROUPS):
             raw[k, g : g + 1, :] = cen[k : k + 1, g * LANES : (g + 1) * LANES]
@@ -114,23 +116,26 @@
 
     pl.semaphore_wait(barrier, plane - 1 + levels - 1 + 1)
 
-    each(width, lambda i: send(row.at[x], row.at[x], sem_px, (y * width + lax.rem(x + i, width), dom)))
-
     feature = lax.rem(r, 4)
     sender = lax.rem(z, classes) == lax.div(r, 4)
     place = lax.div(z, classes)
 
     @pl.when(sender)
     def _():
-        each(levels, lambda i: send(raw.at[feature], pa.at[place], sem_a, level_peer(i)))
+        for i in level_offsets:
+            send(raw.at[feature], pa.at[place], sem_a, level_peer(i))
         pa[place] = raw[feature]
+
+    for i in range(1, width):
+        send(row.at[x], row.at[x], sem_px, (y * width + wrap(x + i, width), dom))
 
     @pl.when(z == r)
     def _():
         error = err[...]
         ad[0] = (MAP_SCALE / (owned * GROUPS * LANES)) / (error * error) / wid[...]
         ad[1] = den[...]
-        each(levels, lambda i: send(ad, ad, sem_ad, level_peer(i)))
+        for i in level_offsets:
+            send(ad, ad, sem_ad, level_peer(i))
 
     if held > 1:
         @pl.when(sender)
@@ -141,7 +146,8 @@
     def _():
         received(pa, sem_a)
 
-    each(reps, lambda i: send(pa, cf.at[c, r], sem_b, rep_peer(i)))
+    for o in rep_offsets:
+        send(pa, cf.at[c, r], sem_b, plane_peer(o)[1])
     cf[c, r] = pa[...]
 
     def source_of(k):
@@ -149,7 +155,7 @@
 
     received(row.at[pl.ds(0, width - 1)], sem_px)
     for i in range(1, height):
-        there = lax.rem(y + i, height)
+        there = wrap(y + i, height)
         to = there * width + x
         out2[i - 1] = row[lax.rem(source_of(to), width)]
         send(out2.at[i - 1], col.at[y], sem_py, (to, dom))
@@ -232,6 +238,7 @@
             h, m, l = split3(jnp.concatenate([xyz, jnp.sum(xyz * xyz, 0, keepdims=True)], 0))
             rows = jnp.concatenate([h, h, m, h, l, m, ones3, zeros5], 0)
             at[t] = rows.T.astype(BF16)
+            ar[t] = rows.astype(BF16)
 
     def pair_features(s):
         for i in range(tiles + 4):
@@ -279,23 +286,43 @@
                 n = t * owned + j
                 for q in range(GROUPS * LANES // chunk):
                     cut = slice(q * chunk, (q + 1) * chunk)
-                    g = jnp.exp2(dot(a, bf[o, :, cut], NN))
-                    total = jnp.sum(g, 0, keepdims=True)
+                    total = jnp.sum(jnp.exp2(dot(a, bf[o, :, cut], NN)), 0, keepdims=True)
                     for i in range(chunk // LANES):
                         k = q * (chunk // LANES) + i
                         part[n, k : k + 1, :] = total[:, i * LANES : (i + 1) * LANES]
-                    h, l = halves(g)
-                    g2[n, 0:LANES, cut] = h
-                    g2[n, LANES : 2 * LANES, cut] = l
             return carry
 
         lax.fori_loop(0, tiles, step, 0)
+
+    def turn_features():
+        def step(o, carry):
+            for g in range(GROUPS):
+                cut = slice(g * LANES, (g + 1) * LANES)
+                bt[o, cut, :] = bf[o, :, cut].astype(F32).T.astype(BF16)
+            return carry
+
+        lax.fori_loop(0, doms, step, 0)
+
+    def gaussian_pass(first, last):
+        def step(t, carry):
+            a = ar[t]
+            for j in range(owned):
+                o = owners[t, j]
+                n = t * owned + j
+                for q in range(GROUPS * LANES // chunk):
+                    cut = slice(q * chunk, (q + 1) * chunk)
+                    h, l = halves(jnp.exp2(dot(bt[o, cut, :], a, NN)))
+                    g2[n, cut, 0:LANES] = h
+                    g2[n, cut, LANES : 2 * LANES] = l
+            return carry
+
+        lax.fori_loop(first, last, step, 0)
 
     def force_pass():
         def step(t, carry):
             sums = jnp.zeros((16, 2 * LANES), F32)
             for j in range(owned):
-                sums = sums + dot(qf[owners[t, j]], g2[t * owned + j], NT)
+                sums = sums + dot(qf[owners[t, j]], g2[t * owned + j], NN)
             sums = sums[:, :LANES] + sums[:, LANES:]
             xyz = own[t, 0:3, :]
             force = fp[t, 0:3, :] + pulled(sums, xyz)
@@ -329,43 +356,47 @@
 
         lax.fori_loop(0, plane, gather, 0)
 
-        def scatter(i, s=s):
-            k, to = plane_peer(i)
+        for o in plane_offsets:
+            k, to = plane_peer(o)
             send(d1.at[s, k], r1.at[s, p], sem_1.at[s], to)
-
-        each(plane, scatter)
         r1[s, p] = d1[s, p]
 
         wait_halo(s)
         pair_features(s)
         pair_pass()
+        if s == 0:
+            turn_features()
 
         received(r1.at[s, pl.ds(0, plane - 1)], sem_1.at[s])
         total = jnp.sum(r1[s], 0)
         t1[s] = total
-        each(levels, lambda i, s=s: send(t1.at[s], r2.at[s, z], sem_2.at[s], level_peer(i)))
+        for i in level_offsets:
+            send(t1.at[s], r2.at[s, z], sem_2.at[s], level_peer(i))
         r2[s, z] = total
+        gaussian_pass(0, tiles)
         received(r2.at[s, pl.ds(0, levels - 1)], sem_2.at[s])
         mean = jnp.sum(r2[s], 0) * (1.0 / (owned * tiles * LANES * reps))
         coef = ad[0] * (mean - ad[1])
         cs[s] = coef
-        each(plane, lambda i, s=s: send(cs.at[s], co.at[s, p], sem_3.at[s], plane_peer(i)[1]))
+        for o in plane_offsets:
+            send(cs.at[s], co.at[s, p], sem_3.at[s], plane_peer(o)[1])
         co[s, p] = coef
         if s == STEPS - 1:
             @pl.when(z == r)
             def _(mean=mean):
                 ms[...] = mean
                 omap[...] = mean
-                each(reps, lambda i: send(ms, mm, sem_m, rep_peer(i)))
+                for o in rep_offsets:
+                    send(ms, mm, sem_m, plane_peer(o)[1])
 
         received(co.at[s, pl.ds(0, plane - 1)], sem_3.at[s])
         coefficient_features(s)
         force_pass()
 
     for t in range(tiles):
-        cut = slice(t * LANES, (t + 1) * LANES)
-        opos[0, :, cut] = own[t, 0:3, :]
-        ovel[0, :, cut] = own[t, 4:7, :]
+        for k in range(3):
+            opos[k, t : t + 1, :] = own[t, k : k + 1, :]
+            ovel[k, t : t + 1, :] = own[t, 4 + k : 5 + k, :]
 
     @pl.when(z != r)
     def _():
@@ -426,8 +457,8 @@
     outs = pl.pallas_call(
         functools.partial(kernel, reps, doms, near, owned),
         out_shape=[
-            jax.ShapeDtypeStruct(positions.shape, F32),
-            jax.ShapeDtypeStruct(velocities.shape, F32),
+            jax.ShapeDtypeStruct((3,) + tile, F32),
+            jax.ShapeDtypeStruct((3,) + tile, F32),
             jax.ShapeDtypeStruct(tile, F32),
         ],
         in_specs=[vmem] * 4 + [smem] * 4 + [vmem] * 4 + [smem] * 2,
@@ -444,14 +475,16 @@
             pltpu.VMEM((2, reps, held) + tile, F32),
             pltpu.VMEM((2,) + tile, F32),
             pltpu.VMEM((doms, 32, GROUPS * LANES), BF16),
+            pltpu.VMEM((doms, GROUPS * LANES, 32), BF16),
             pltpu.VMEM((doms, 16, GROUPS * LANES), BF16),
             pltpu.VMEM((GROUPS * 32, LANES), F32),
             pltpu.VMEM((GROUPS * 16, LANES), F32),
             pltpu.VMEM((tiles, LANES, 32), BF16),
+            pltpu.VMEM((tiles, 32, LANES), BF16),
             pltpu.VMEM((tiles + 5, 32, LANES), BF16),
             pltpu.VMEM((tiles + 5, 16, LANES), BF16),
             pltpu.VMEM((tiles,) + tile, F32),
-            pltpu.VMEM((slots, 2 * LANES, GROUPS * LANES), BF16),
+            pltpu.VMEM((slots, GROUPS * LANES, 2 * LANES), BF16),
             pltpu.VMEM((slots + 1,) + tile, F32),
             pltpu.VMEM((STEPS, plane) + tile, F32),
             pltpu.VMEM((STEPS, plane) + tile, F32),
@@ -466,13 +499,13 @@
             pair_sems,
         ],
         compiler_params=pltpu.CompilerParams(
-            collective_id=0, has_side_effects=True, vmem_limit_bytes=44 * 1024 * 1024
+            collective_id=0, has_side_effects=True, vmem_limit_bytes=52 * 1024 * 1024
         ),
     )(
-        positions, velocities, square(charge), square(inverse_mass), pair_tiles, halo_tiles, owners,
+        positions.reshape((3,) + tile), velocities.reshape((3,) + tile), square(charge), square(inverse_mass), pair_tiles, halo_tiles, owners,
         inv, centres, square(widths), square(map_density), square(map_error), partner, decision,
     )
-    return outs[0], outs[1], outs[2].reshape(GROUPS * LANES)
+    return outs[0].reshape(positions.shape), outs[1].reshape(velocities.shape), outs[2].reshape(GROUPS * LANES)
 
 
 def solution(mesh):

time: 99 us -> 93.6 us (0.945)
  Pallas kernels: 93.9 us -> 84.9 us
  local copies, waits for them, and re-layouts: 3.97 us -> 7.43 us
    pallas_call x1, Pallas kernels: 93.9 us -> 84.9 us  [local(): pl.pallas_call(functools.partial(kernel, reps, doms, near, owned), out_sh...]
    unnamed x32 -> x28, local copies, waits for them, and re-layouts: 3.89 us -> 7.35 us
where the time goes in v2:
time: 93.6 us; the launch traced here: 93.2 us
  Pallas kernels  84.9 us (91%)
  local copies, waits for them, and re-layouts  7.43 us (8%)
    pallas_call x1, Pallas kernels, local(): pl.pallas_call(functools.partial(kernel, reps, doms, near, owned), out_sh...  84.9 us
    unnamed x28, local copies, waits for them, and re-layouts  7.35 us

profile of v2, /device:TPU:1, one launch (start us, length us, event | category | flops | bytes accessed | tf_op | source)
XLA Modules:
  0.0 93.2 jit_solution(4476175840254381017)
XLA Ops:
  0.6 0.0 copy-start.10
  0.6 0.0 copy-start.11
  0.7 0.0 copy-start.3
  0.7 0.0 copy-start
  0.7 0.8 copy.25.owners
  1.5 0.1 eq.15
  1.5 0.1 select_reduce_fusion.1
  1.7 0.0 copy-start.9
  1.7 0.0 copy-done.10
  1.7 0.0 copy-done.11
  1.7 0.0 copy-done.3
  1.7 0.0 copy-done
  1.7 0.0 copy-done.1
  1.8 0.6 copy-done.9
  2.4 0.7 copy-done.2
  3.1 0.7 copy-done.4
  3.8 0.7 copy-done.5
  4.4 0.7 copy-done.6
  5.1 0.7 copy-done.7
  5.8 0.7 copy-done.8
  6.5 84.9 %shard_map.148 = (f32[3,8,128]{2,1,0:T(8,128)S(1)}, f32[3,8,128]{2,1,0:T(8,128)S(1)}, f32[8,128]{1,0:T(8,128)S(1)}) custom-call(f32[3,8,128]{2,1,0:T(8,128)S(1)} %bitcast.14, f32[3,8,128]{2,1,0:T(8,128)S(1)} %bitcast.15, f32[8,128]{1,0:T(8,128)S(1)} %bitcast.18, f32[8,128]{1,0:T(8,128)S(1)} %bitcast.19, s32[8,6]{1,0:T(8,128)S(1)} %copy-done.5, ...), custom_call_target="tpu_custom_call" | custom-call | tf_op jit(solution)/shard_map/pallas_call | solution.py:457
  91.4 0.6 copy.31
  92.0 0.6 copy.32
  92.6 0.6 copy.33
  (9 shorter events, 0.0 us)
Async XLA Ops:
  0.6 1.1 %copy-start.10 = (s32[16]{0:T(128)S(1)}, s32[16]{0:T(128)}, u32[]{:S(2)}) copy-start(s32[16]{0:T(128)} %partner.1) | copy-start | bytes 196
  0.6 1.1 %copy-start.11 = (s32[16]{0:T(128)S(1)}, s32[16]{0:T(128)}, u32[]{:S(2)}) copy-start(s32[16]{0:T(128)} %decision.1) | copy-start | bytes 196
  0.7 1.1 %copy-start.3 = (f32[1024]{0:T(1024)S(1)}, f32[1024]{0:T(1024)}, u32[]{:S(2)}) copy-start(f32[1024]{0:T(1024)} %param.15) | copy-start | bytes 12292
  0.7 1.1 %copy-start = (f32[3,1024]{1,0:T(4,128)S(1)}, f32[3,1024]{1,0:T(4,128)}, u32[]{:S(2)}) copy-start(f32[3,1024]{1,0:T(4,128)} %cen.1) | copy-start | bytes 36868
  0.7 1.1 %copy-start.1 = (f32[1,3,1024]{2,0,1:T(1,128)S(1)}, f32[1,3,1024]{2,0,1:T(1,128)}, u32[]{:S(2)}) copy-start(f32[1,3,1024]{2,0,1:T(1,128)} %param.13) | copy-start | bytes 36868
  1.7 0.7 copy-start.9
  2.4 0.7 copy-start.2
  3.1 0.7 copy-start.4
  3.8 0.7 copy-start.5
  4.4 0.7 copy-start.6
  5.1 0.7 copy-start.7
  5.8 0.7 copy-start.8

commit v3 on v2

--- a/solution.py
+++ b/solution.py
@@ -193,40 +193,45 @@
         return cx, cy, cz, w
 
     def component_features(cc):
-        def step(zz, carry):
+        def one(zz, u):
             cx, cy, cz, w = basis(zz, cc)
             iw = LOG2E / w
             half = -0.5 * iw
             terms = [split3(v) for v in (cx * iw, cy * iw, cz * iw, half)]
             for group, level in enumerate((0, 1, 0, 2, 0, 1)):
                 for f in range(4):
-                    scr[pl.ds(group * 4 + f, GROUPS, stride=32), :] = terms[f][level]
+                    scr[u, pl.ds(group * 4 + f, GROUPS, stride=32), :] = terms[f][level]
             for level, v in enumerate(split3(half * (cx * cx + cy * cy + cz * cz))):
-                scr[pl.ds(24 + level, GROUPS, stride=32), :] = v
-            o = 2 * zz + cc
-            for g in range(GROUPS):
-                bf[o, :, g * LANES : (g + 1) * LANES] = scr[g * 32 : (g + 1) * 32, :].astype(BF16)
-            return carry
-
-        lax.fori_loop(0, levels, step, 0)
+                scr[u, pl.ds(24 + level, GROUPS, stride=32), :] = v
+
+        def step(i, carry):
+            for u in range(2):
+                one(2 * i + u, u)
+            for u in range(2):
+                o = 2 * (2 * i + u) + cc
+                for g in range(GROUPS):
+                    bf[o, :, g * LANES : (g + 1) * LANES] = scr[u, g * 32 : (g + 1) * 32, :].astype(BF16)
+            return carry
+
+        lax.fori_loop(0, levels // 2, step, 0)
 
     def coefficient_features(s):
-        def one(zz, cc):
+        def one(zz, cc, u):
             cx, cy, cz, _ = basis(zz, cc)
-            o = 2 * zz + cc
-            coef = co[s, o]
+            coef = co[s, 2 * zz + cc]
             for f, v in enumerate((coef, coef * cx, coef * cy, coef * cz)):
                 for level, piece in enumerate(split3(v)):
-                    scr2[pl.ds(level * 4 + f, GROUPS, stride=16), :] = piece
-            for g in range(GROUPS):
-                qf[o, :, g * LANES : (g + 1) * LANES] = scr2[g * 16 : (g + 1) * 16, :].astype(BF16)
-
-        def step(zz, carry):
-            one(zz, 0)
-            one(zz, 1)
-            return carry
-
-        lax.fori_loop(0, levels, step, 0)
+                    scr2[u, pl.ds(level * 4 + f, GROUPS, stride=16), :] = piece
+
+        def step(i, carry):
+            for u in range(4):
+                one(2 * i + u // 2, u % 2, u)
+            for u in range(4):
+                for g in range(GROUPS):
+                    qf[4 * i + u, :, g * LANES : (g + 1) * LANES] = scr2[u, g * 16 : (g + 1) * 16, :].astype(BF16)
+            return carry
+
+        lax.fori_loop(0, doms // 4, step, 0)
 
     ones3 = jnp.ones((3, LANES), F32)
     zeros4 = jnp.zeros((4, LANES), F32)
@@ -279,7 +284,7 @@
     chunk = 256
 
     def intersection_pass():
-        def step(t, carry):
+        def one(t):
             a = at[t]
             for j in range(owned):
                 o = owners[t, j]
@@ -290,9 +295,13 @@
                     for i in range(chunk // LANES):
                         k = q * (chunk // LANES) + i
                         part[n, k : k + 1, :] = total[:, i * LANES : (i + 1) * LANES]
-            return carry
-
-        lax.fori_loop(0, tiles, step, 0)
+
+        def step(i, carry):
+            one(2 * i)
+            one(2 * i + 1)
+            return carry
+
+        lax.fori_loop(0, tiles // 2, step, 0)
 
     def turn_features():
         def step(o, carry):
@@ -319,7 +328,7 @@
         lax.fori_loop(first, last, step, 0)
 
     def force_pass():
-        def step(t, carry):
+        def one(t):
             sums = jnp.zeros((16, 2 * LANES), F32)
             for j in range(owned):
                 sums = sums + dot(qf[owners[t, j]], g2[t * owned + j], NN)
@@ -329,9 +338,13 @@
             v = own[t, 4:7, :] + TIME_STEP * own[t, 7:8, :] * force
             own[t, 4:7, :] = v
             own[t, 0:3, :] = xyz + TIME_STEP * v
-            return carry
-
-        lax.fori_loop(0, tiles, step, 0)
+
+        def step(i, carry):
+            one(2 * i)
+            one(2 * i + 1)
+            return carry
+
+        lax.fori_loop(0, tiles // 2, step, 0)
 
     received(cf.at[c, pl.ds(0, reps - 1)], sem_b)
     send(cf.at[c], cf.at[c], sem_c, other_core)
@@ -350,11 +363,8 @@
             atom_features()
         intersection_pass()
 
-        def gather(k, carry, s=s):
+        for k in range(plane):
             d1[s, k] = part[inv[0, k]] + part[inv[1, k]]
-            return carry
-
-        lax.fori_loop(0, plane, gather, 0)
 
         for o in plane_offsets:
             k, to = plane_peer(o)
@@ -364,8 +374,6 @@
         wait_halo(s)
         pair_features(s)
         pair_pass()
-        if s == 0:
-            turn_features()
 
         received(r1.at[s, pl.ds(0, plane - 1)], sem_1.at[s])
         total = jnp.sum(r1[s], 0)
@@ -373,7 +381,10 @@
         for i in level_offsets:
             send(t1.at[s], r2.at[s, z], sem_2.at[s], level_peer(i))
         r2[s, z] = total
-        gaussian_pass(0, tiles)
+        if s == 0:
+            turn_features()
+        early = 4 if s == 0 else 6
+        gaussian_pass(0, early)
         received(r2.at[s, pl.ds(0, levels - 1)], sem_2.at[s])
         mean = jnp.sum(r2[s], 0) * (1.0 / (owned * tiles * LANES * reps))
         coef = ad[0] * (mean - ad[1])
@@ -389,6 +400,7 @@
                 for o in rep_offsets:
                     send(ms, mm, sem_m, plane_peer(o)[1])
 
+        gaussian_pass(early, tiles)
         received(co.at[s, pl.ds(0, plane - 1)], sem_3.at[s])
         coefficient_features(s)
         force_pass()
@@ -477,8 +489,8 @@
             pltpu.VMEM((doms, 32, GROUPS * LANES), BF16),
             pltpu.VMEM((doms, GROUPS * LANES, 32), BF16),
             pltpu.VMEM((doms, 16, GROUPS * LANES), BF16),
-            pltpu.VMEM((GROUPS * 32, LANES), F32),
-            pltpu.VMEM((GROUPS * 16, LANES), F32),
+            pltpu.VMEM((2, GROUPS * 32, LANES), F32),
+            pltpu.VMEM((4, GROUPS * 16, LANES), F32),
             pltpu.VMEM((tiles, LANES, 32), BF16),
             pltpu.VMEM((tiles, 32, LANES), BF16),
             pltpu.VMEM((tiles + 5, 32, LANES), BF16),

time: 93.6 us -> 87.8 us (0.938)
  Pallas kernels: 84.9 us -> 79.1 us
    pallas_call x1, Pallas kernels: 84.9 us -> 79.1 us  [local(): pl.pallas_call(functools.partial(kernel, reps, doms, near, owned), out_sh...]
where the time goes in v3:
time: 87.8 us; the launch traced here: 87.4 us
  Pallas kernels  79.1 us (90%)
  local copies, waits for them, and re-layouts  7.43 us (8%)
    pallas_call x1, Pallas kernels, local(): pl.pallas_call(functools.partial(kernel, reps, doms, near, owned), out_sh...  79.1 us
    unnamed x28, local copies, waits for them, and re-layouts  7.35 us

profile of v3, /device:TPU:1, one launch (start us, length us, event | category | flops | bytes accessed | tf_op | source)
XLA Modules:
  0.0 87.4 jit_solution(17405650503480206983)
XLA Ops:
  0.6 0.0 copy-start.10
  0.6 0.0 copy-start.11
  0.7 0.0 copy-start.3
  0.7 0.0 copy-start
  0.7 0.8 copy.25.owners
  1.5 0.1 eq.15
  1.5 0.1 select_reduce_fusion.1
  1.7 0.0 copy-start.9
  1.7 0.0 copy-done.10
  1.7 0.0 copy-done.11
  1.7 0.0 copy-done.3
  1.7 0.0 copy-done
  1.7 0.0 copy-done.1
  1.8 0.6 copy-done.9
  2.4 0.7 copy-done.2
  3.1 0.7 copy-done.4
  3.8 0.7 copy-done.5
  4.4 0.7 copy-done.6
  5.1 0.7 copy-done.7
  5.8 0.7 copy-done.8
  6.5 79.1 %shard_map.148 = (f32[3,8,128]{2,1,0:T(8,128)S(1)}, f32[3,8,128]{2,1,0:T(8,128)S(1)}, f32[8,128]{1,0:T(8,128)S(1)}) custom-call(f32[3,8,128]{2,1,0:T(8,128)S(1)} %bitcast.14, f32[3,8,128]{2,1,0:T(8,128)S(1)} %bitcast.15, f32[8,128]{1,0:T(8,128)S(1)} %bitcast.18, f32[8,128]{1,0:T(8,128)S(1)} %bitcast.19, s32[8,6]{1,0:T(8,128)S(1)} %copy-done.5, ...), custom_call_target="tpu_custom_call" | custom-call | tf_op jit(solution)/shard_map/pallas_call | solution.py:469
  85.6 0.6 copy.31
  86.2 0.6 copy.32
  86.8 0.6 copy.33
  (9 shorter events, 0.0 us)
Async XLA Ops:
  0.6 1.1 %copy-start.10 = (s32[16]{0:T(128)S(1)}, s32[16]{0:T(128)}, u32[]{:S(2)}) copy-start(s32[16]{0:T(128)} %partner.1) | copy-start | bytes 196
  0.6 1.1 %copy-start.11 = (s32[16]{0:T(128)S(1)}, s32[16]{0:T(128)}, u32[]{:S(2)}) copy-start(s32[16]{0:T(128)} %decision.1) | copy-start | bytes 196
  0.7 1.1 %copy-start.3 = (f32[1024]{0:T(1024)S(1)}, f32[1024]{0:T(1024)}, u32[]{:S(2)}) copy-start(f32[1024]{0:T(1024)} %param.15) | copy-start | bytes 12292
  0.7 1.1 %copy-start = (f32[3,1024]{1,0:T(4,128)S(1)}, f32[3,1024]{1,0:T(4,128)}, u32[]{:S(2)}) copy-start(f32[3,1024]{1,0:T(4,128)} %cen.1) | copy-start | bytes 36868
  0.7 1.1 %copy-start.1 = (f32[1,3,1024]{2,0,1:T(1,128)S(1)}, f32[1,3,1024]{2,0,1:T(1,128)}, u32[]{:S(2)}) copy-start(f32[1,3,1024]{2,0,1:T(1,128)} %param.13) | copy-start | bytes 36868
  1.7 0.7 copy-start.9
  2.4 0.7 copy-start.2
  3.1 0.7 copy-start.4
  3.8 0.7 copy-start.5
  4.4 0.7 copy-start.6
  5.1 0.7 copy-start.7
  5.8 0.7 copy-start.8

commit v4 on v3

--- a/solution.py
+++ b/solution.py
@@ -34,11 +34,11 @@
 
 def kernel(
     reps, doms, near, owned,
-    pos, vel, charge, imass, pair, halo, owners, inv, cen, wid, den, err, partner, decision,
+    pos, vel, charge_in, imass_in, pair, halo, owners, inv, cen_in, wid, den_in, err_in, partner, decision,
     opos, ovel, omap,
-    row, out2, col, own, hs, hr, raw, pa, cf, ad, bf, bt, qf, scr, scr2, at, ar, pb, pq, fp, g2, part,
+    charge, imass, cen, den, err, row, out2, col, own, hs, hr, raw, pa, cf, ad, bf, bt, qf, scr, scr2, at, ar, pb, pq, fp, g2, part,
     d1, r1, t1, r2, cs, co, ms, mm,
-    sem_px, sem_py, sem_a, sem_ad, sem_b, sem_c, sem_h, sem_hs, sem_1, sem_2, sem_3, sem_m,
+    sem_px, sem_py, sem_a, sem_ad, sem_b, sem_c, sem_h, sem_hs, sem_1, sem_2, sem_3, sem_m, sem_in,
 ):
     width = math.isqrt(reps)
     height = reps // width
@@ -104,15 +104,21 @@
         greet(plane_peer(o)[1])
     greet((r, jnp.where(c == 0, below, above)))
 
-    row[x, 0:3] = pos[...]
-    row[x, 3:6] = vel[...]
+    wanted = (
+        (cen_in, cen), (wid, raw.at[3]), (pos, row.at[x, pl.ds(0, 3)]), (vel, row.at[x, pl.ds(3, 3)]),
+        (charge_in, charge), (imass_in, imass), (den_in, den), (err_in, err),
+    )
+    loads = [pltpu.make_async_copy(src, dst, sem_in.at[i]) for i, (src, dst) in enumerate(wanted)]
+    for load in loads:
+        load.start()
+    scr[...] = jnp.zeros_like(scr)
+    scr2[...] = jnp.zeros_like(scr2)
+    part[slots] = jnp.zeros((GROUPS, LANES), F32)
+    for load in loads:
+        load.wait()
     for k in range(3):
         for g in range(GROUPS):
             raw[k, g : g + 1, :] = cen[k : k + 1, g * LANES : (g + 1) * LANES]
-    raw[3] = wid[...]
-    scr[...] = jnp.zeros_like(scr)
-    scr2[...] = jnp.zeros_like(scr2)
-    part[slots] = jnp.zeros((GROUPS, LANES), F32)
 
     pl.semaphore_wait(barrier, plane - 1 + levels - 1 + 1)
 
@@ -132,7 +138,7 @@
     @pl.when(z == r)
     def _():
         error = err[...]
-        ad[0] = (MAP_SCALE / (owned * GROUPS * LANES)) / (error * error) / wid[...]
+        ad[0] = (MAP_SCALE / (owned * GROUPS * LANES)) / (error * error) / raw[3]
         ad[1] = den[...]
         for i in level_offsets:
             send(ad, ad, sem_ad, level_peer(i))
@@ -287,7 +293,7 @@
         def one(t):
             a = at[t]
             for j in range(owned):
-                o = owners[t, j]
+                o = owners[j, t]
                 n = t * owned + j
                 for q in range(GROUPS * LANES // chunk):
                     cut = slice(q * chunk, (q + 1) * chunk)
@@ -316,7 +322,7 @@
         def step(t, carry):
             a = ar[t]
             for j in range(owned):
-                o = owners[t, j]
+                o = owners[j, t]
                 n = t * owned + j
                 for q in range(GROUPS * LANES // chunk):
                     cut = slice(q * chunk, (q + 1) * chunk)
@@ -331,7 +337,7 @@
         def one(t):
             sums = jnp.zeros((16, 2 * LANES), F32)
             for j in range(owned):
-                sums = sums + dot(qf[owners[t, j]], g2[t * owned + j], NN)
+                sums = sums + dot(qf[owners[j, t]], g2[t * owned + j], NN)
             sums = sums[:, :LANES] + sums[:, LANES:]
             xyz = own[t, 0:3, :]
             force = fp[t, 0:3, :] + pulled(sums, xyz)
@@ -437,6 +443,14 @@
         sent(co.at[s, pl.ds(0, plane - 1)], sem_3.at[s])
 
 
+def write_out(a, b, c, x, y, z, sems):
+    moves = [pltpu.make_async_copy(u, v, sems.at[i]) for i, (u, v) in enumerate(((a, x), (b, y), (c, z)))]
+    for move in moves:
+        move.start()
+    for move in moves:
+        move.wait()
+
+
 def local(
     positions, velocities, charge, inverse_mass, pair_tiles, halo_tiles, owners,
     centres, widths, map_density, map_error, partner, decision,
@@ -452,10 +466,11 @@
     held = levels // (reps // 4)
     plane = 2 * reps
 
-    named = owners.reshape(1, slots) == jnp.arange(doms, dtype=jnp.int32)[:, None]
-    ids = jnp.arange(slots, dtype=jnp.int32)[None, :]
-    first = jnp.min(jnp.where(named, ids, slots), 1)
-    last = jnp.max(jnp.where(named, ids, -1), 1)
+    turned = owners.T
+    named = turned[None] == jnp.arange(doms, dtype=jnp.int32)[:, None, None]
+    ids = jnp.arange(tiles, dtype=jnp.int32)[None, None, :] * owned + jnp.arange(owned, dtype=jnp.int32)[None, :, None]
+    first = jnp.min(jnp.where(named, ids, slots), (1, 2))
+    last = jnp.max(jnp.where(named, ids, -1), (1, 2))
     inv = jnp.stack([first, jnp.where(last > first, last, slots)])
 
     def square(v):
@@ -463,6 +478,7 @@
 
     tile = (GROUPS, LANES)
     vmem = pl.BlockSpec(memory_space=pltpu.VMEM)
+    hbm = pl.BlockSpec(memory_space=pltpu.HBM)
     smem = pl.BlockSpec(memory_space=pltpu.SMEM)
     pair_sems = pltpu.SemaphoreType.DMA((2,))
     step_sems = pltpu.SemaphoreType.DMA((STEPS, 2))
@@ -473,9 +489,14 @@
             jax.ShapeDtypeStruct((3,) + tile, F32),
             jax.ShapeDtypeStruct(tile, F32),
         ],
-        in_specs=[vmem] * 4 + [smem] * 4 + [vmem] * 4 + [smem] * 2,
+        in_specs=[hbm] * 4 + [smem] * 4 + [hbm] * 4 + [smem] * 2,
         out_specs=[vmem] * 3,
         scratch_shapes=[
+            pltpu.VMEM(tile, F32),
+            pltpu.VMEM(tile, F32),
+            pltpu.VMEM((3, GROUPS * LANES), F32),
+            pltpu.VMEM(tile, F32),
+            pltpu.VMEM(tile, F32),
             pltpu.VMEM((width, 6) + tile, F32),
             pltpu.VMEM((height - 1, 6) + tile, F32),
             pltpu.VMEM((height, 6) + tile, F32),
@@ -509,14 +530,22 @@
             pair_sems, pair_sems, pair_sems, pair_sems, pair_sems, pair_sems,
             step_sems, step_sems, step_sems, step_sems, step_sems,
             pair_sems,
+            pltpu.SemaphoreType.DMA((8,)),
         ],
         compiler_params=pltpu.CompilerParams(
-            collective_id=0, has_side_effects=True, vmem_limit_bytes=52 * 1024 * 1024
+            collective_id=0, has_side_effects=True, vmem_limit_bytes=64 * 1024 * 1024
         ),
     )(
-        positions.reshape((3,) + tile), velocities.reshape((3,) + tile), square(charge), square(inverse_mass), pair_tiles, halo_tiles, owners,
+        positions.reshape((3,) + tile), velocities.reshape((3,) + tile), square(charge), square(inverse_mass), pair_tiles, halo_tiles, turned,
         inv, centres, square(widths), square(map_density), square(map_error), partner, decision,
     )
+    outs = pl.pallas_call(
+        write_out,
+        out_shape=[jax.ShapeDtypeStruct(o.shape, F32) for o in outs],
+        in_specs=[vmem] * 3,
+        out_specs=[hbm] * 3,
+        scratch_shapes=[pltpu.SemaphoreType.DMA((3,))],
+    )(*outs)
     return outs[0].reshape(positions.shape), outs[1].reshape(velocities.shape), outs[2].reshape(GROUPS * LANES)
 
 

time: 87.8 us -> 83.6 us (0.952)
  local copies, waits for them, and re-layouts: 7.43 us -> 0.65 us
  Pallas kernels: 79.1 us -> 81.3 us
    unnamed x28 -> x2, local copies, waits for them, and re-layouts: 7.35 us -> 0.65 us
    pallas_call x0 -> x1, Pallas kernels: none -> 1.36 us  [local(): pl.pallas_call(write_out, out_shape=[jax.ShapeDtypeStruct(o.shape, F32) f...]
where the time goes in v4:
time: 83.6 us; the launch traced here: 83.3 us
  Pallas kernels  81.3 us (97%)
    pallas_call x1, Pallas kernels, local(): pl.pallas_call(functools.partial(kernel, reps, doms, near, owned), out_sh...  79.9 us

profile of v4, /device:TPU:1, one launch (start us, length us, event | category | flops | bytes accessed | tf_op | source)
XLA Modules:
  0.0 83.3 jit_solution(8704123113592161597)
XLA Ops:
  0.6 0.0 copy-start
  0.7 0.7 copy-done
  1.3 0.1 select_reduce_fusion.1
  1.4 0.6 pad_add_fusion.inv
  2.0 79.9 %shard_map.148 = (f32[3,8,128]{2,1,0:T(8,128)}, f32[3,8,128]{2,1,0:T(8,128)}, f32[8,128]{1,0:T(8,128)}) custom-call(f32[3,8,128]{2,1,0:T(8,128)} %bitcast.15, f32[3,8,128]{2,1,0:T(8,128)} %bitcast.16, f32[8,128]{1,0:T(8,128)} %bitcast.19, f32[8,128]{1,0:T(8,128)} %bitcast.20, s32[8,6]{1,0:T(8,128)} %pair.1, s32[1,2,2]{2,1,0:T(2,128)} %halo.1, ...), custom_call_target="tpu_custom_call" | custom-call | tf_op jit(solution)/shard_map/pallas_call | solution.py:485
  81.9 1.4 %shard_map.149 = (f32[3,8,128]{2,1,0:T(8,128)}, f32[3,8,128]{2,1,0:T(8,128)}, f32[8,128]{1,0:T(8,128)}) custom-call(f32[3,8,128]{2,1,0:T(8,128)} %get-tuple-element.9.a, f32[3,8,128]{2,1,0:T(8,128)} %get-tuple-element.10.b, f32[8,128]{1,0:T(8,128)} %get-tuple-element.11.c), custom_call_target="tpu_custom_call" | custom-call | tf_op jit(solution)/shard_map/pallas_call | solution.py:542
  (3 shorter events, 0.0 us)
Async XLA Ops:
  0.6 0.7 copy-start

commit v5 on v4

--- a/solution.py
+++ b/solution.py
@@ -34,9 +34,9 @@
 
 def kernel(
     reps, doms, near, owned,
-    pos, vel, charge_in, imass_in, pair, halo, owners, inv, cen_in, wid, den_in, err_in, partner, decision,
+    pos, vel, charge_in, imass_in, pair, halo, owners, cen_in, wid, den_in, err_in, partner, decision,
     opos, ovel, omap,
-    charge, imass, cen, den, err, row, out2, col, own, hs, hr, raw, pa, cf, ad, bf, bt, qf, scr, scr2, at, ar, pb, pq, fp, g2, part,
+    inv, charge, imass, cen, den, err, row, out2, col, own, hs, hr, raw, pa, cf, ad, bf, bt, qf, scr, scr2, at, ar, pb, pq, fp, g2, part,
     d1, r1, t1, r2, cs, co, ms, mm,
     sem_px, sem_py, sem_a, sem_ad, sem_b, sem_c, sem_h, sem_hs, sem_1, sem_2, sem_3, sem_m, sem_in,
 ):
@@ -114,6 +114,19 @@
     scr[...] = jnp.zeros_like(scr)
     scr2[...] = jnp.zeros_like(scr2)
     part[slots] = jnp.zeros((GROUPS, LANES), F32)
+
+    def find(k, carry):
+        one, two = slots, slots
+        for t in range(tiles):
+            for j in range(owned):
+                hit = owners[j, t] == k
+                two = jnp.where(hit, one, two)
+                one = jnp.where(hit, t * owned + j, one)
+        inv[0, k] = jnp.asarray(one, jnp.int32)
+        inv[1, k] = jnp.asarray(two, jnp.int32)
+        return carry
+
+    lax.fori_loop(0, doms, find, 0)
     for load in loads:
         load.wait()
     for k in range(3):
@@ -466,13 +479,6 @@
     held = levels // (reps // 4)
     plane = 2 * reps
 
-    turned = owners.T
-    named = turned[None] == jnp.arange(doms, dtype=jnp.int32)[:, None, None]
-    ids = jnp.arange(tiles, dtype=jnp.int32)[None, None, :] * owned + jnp.arange(owned, dtype=jnp.int32)[None, :, None]
-    first = jnp.min(jnp.where(named, ids, slots), (1, 2))
-    last = jnp.max(jnp.where(named, ids, -1), (1, 2))
-    inv = jnp.stack([first, jnp.where(last > first, last, slots)])
-
     def square(v):
         return v.reshape(GROUPS, LANES)
 
@@ -489,9 +495,10 @@
             jax.ShapeDtypeStruct((3,) + tile, F32),
             jax.ShapeDtypeStruct(tile, F32),
         ],
-        in_specs=[hbm] * 4 + [smem] * 4 + [hbm] * 4 + [smem] * 2,
+        in_specs=[hbm] * 4 + [smem] * 3 + [hbm] * 4 + [smem] * 2,
         out_specs=[vmem] * 3,
         scratch_shapes=[
+            pltpu.SMEM((2, doms), jnp.int32),
             pltpu.VMEM(tile, F32),
             pltpu.VMEM(tile, F32),
             pltpu.VMEM((3, GROUPS * LANES), F32),
@@ -536,8 +543,8 @@
             collective_id=0, has_side_effects=True, vmem_limit_bytes=64 * 1024 * 1024
         ),
     )(
-        positions.reshape((3,) + tile), velocities.reshape((3,) + tile), square(charge), square(inverse_mass), pair_tiles, halo_tiles, turned,
-        inv, centres, square(widths), square(map_density), square(map_error), partner, decision,
+        positions.reshape((3,) + tile), velocities.reshape((3,) + tile), square(charge), square(inverse_mass), pair_tiles, halo_tiles, owners.T,
+        centres, square(widths), square(map_density), square(map_error), partner, decision,
     )
     outs = pl.pallas_call(
         write_out,

time: 83.6 us -> 82.1 us (0.982)
  no operation moved by 1% of the time
where the time goes in v5:
time: 82.1 us; the launch traced here: 81.9 us
  Pallas kernels  81.3 us (99%)
    pallas_call x1, Pallas kernels, local(): pl.pallas_call(functools.partial(kernel, reps, doms, near, owned), out_sh...  79.9 us

profile of v5, /device:TPU:1, one launch (start us, length us, event | category | flops | bytes accessed | tf_op | source)
XLA Modules:
  0.0 81.9 jit_solution(9584565569610066054)
XLA Ops:
  0.6 79.9 %shard_map.148 = (f32[3,8,128]{2,1,0:T(8,128)}, f32[3,8,128]{2,1,0:T(8,128)}, f32[8,128]{1,0:T(8,128)}) custom-call(f32[3,8,128]{2,1,0:T(8,128)} %bitcast.11, f32[3,8,128]{2,1,0:T(8,128)} %bitcast.12, f32[8,128]{1,0:T(8,128)} %bitcast.13, f32[8,128]{1,0:T(8,128)} %bitcast.14, s32[8,6]{1,0:T(8,128)} %pair.1, s32[1,2,2]{2,1,0:T(2,128)} %halo.1, ...), custom_call_target="tpu_custom_call" | custom-call | tf_op jit(solution)/shard_map/pallas_call | solution.py:491
  80.5 1.4 %shard_map.149 = (f32[3,8,128]{2,1,0:T(8,128)}, f32[3,8,128]{2,1,0:T(8,128)}, f32[8,128]{1,0:T(8,128)}) custom-call(f32[3,8,128]{2,1,0:T(8,128)} %get-tuple-element.9.a, f32[3,8,128]{2,1,0:T(8,128)} %get-tuple-element.10.b, f32[8,128]{1,0:T(8,128)} %get-tuple-element.11.c), custom_call_target="tpu_custom_call" | custom-call | tf_op jit(solution)/shard_map/pallas_call | solution.py:549
